TPU v7x, 32 devices: a whole 2x2x4 slice. The times are simulated.
32 devices in a mesh: dom: 8 (over z, y), member: 4 (over x, core).
Axes of the slice: x: 2, y: 2, z: 4, core: 2. Of those that a mesh axis runs over, the one named last changes fastest.
Arguments:
- state: float32 [32, 768, 512], P('member', 'dom'), may hold values from -6 to 6
- noise: bfloat16 [8, 32, 768, 512], P(None, 'member', 'dom'), may hold values from -1.75 to 1.75
- w_local: bfloat16 [512, 512], replicated, may hold values from -0.25 to 0.25
- conn_weight: float32 [16, 768], P(None, 'dom'), may hold values from -1.75 to 1.75
- conn_index: int32 [16, 768], P(None, 'dom'), may hold values from 0 to 127, as said below
- boundary: int32 [8, 8], P('dom'), may hold values from 0 to 95, as said below
- send_pos: int32 [8, 8, 4], replicated, may hold values from 0 to 7
- readout: float32 [512], replicated, may hold values from -0.25 to 0.25
- observed: int32 [8, 64], P('dom'), may hold values from 0 to 95, as said below
- obs_value: float32 [8, 64], P('dom'), may hold values from -6 to 6
- obs_var: float32 [8, 64], P('dom'), may hold values from 0.1 to 1
- obs_pert: float32 [32, 8, 64], P('member', 'dom'), may hold values from -6 to 6
Outputs:
- analysis: float32 [32, 768, 512], P('member', 'dom')
Inputs may be any that keep to these rules, and one draw needn't show every extreme that they name: `conn_index`: each voxel's inputs number 12 rows of its own part (below 96) and 4 received slots; every slot is read by some voxel of its part. Each part's boundary rows are distinct. Each part's observed rows are distinct.
All inputs are finite; a program needn't handle non-finite values.
Results may differ from a plain program's by a relative error of at most 0.025.
Values may be sent and summed in bfloat16 or wider, within the bound.
A program may use at most 64 MiB of HBM per device.

v0:
```python
import jax
import jax.numpy as jnp
from jax import lax
from jax.sharding import PartitionSpec as P

RELAX_RATE = 0.5


def per_device(
    state,
    noise,
    w_local,
    conn_weight,
    conn_index,
    boundary,
    send_pos,
    readout,
    observed,
    obs_value,
    obs_var,
    obs_pert,
):
    mem_local, vox_local, width = state.shape
    parts_count = lax.axis_size("dom")
    part_index = lax.axis_index("dom")
    slot_count = send_pos.shape[2]
    table_rows = vox_local + parts_count * slot_count
    onehot = conn_index[:, :, None] == jnp.arange(table_rows, dtype=jnp.int32)[None, None, :]
    conn_matrix = jnp.sum(jnp.where(onehot, conn_weight[:, :, None], 0.0), axis=0)
    conn_high = conn_matrix.astype(jnp.bfloat16)
    conn_low = (conn_matrix - conn_high.astype(jnp.float32)).astype(jnp.bfloat16)
    own_sends = lax.dynamic_index_in_dim(send_pos, part_index, 0, keepdims=False)
    current = state
    for step_index in range(noise.shape[0]):
        rate = jnp.tanh(current).astype(jnp.bfloat16)
        send_rows = jnp.take(boundary[0], own_sends.reshape(-1), axis=0)
        outgoing = jnp.take(rate, send_rows, axis=1)
        received = lax.all_to_all(outgoing, "dom", split_axis=1, concat_axis=1, tiled=True)
        table = jnp.concatenate([rate, received], axis=1)
        drive = jnp.einsum("vu,mus->mvs", conn_high, table, preferred_element_type=jnp.float32)
        drive = drive + jnp.einsum(
            "vu,mus->mvs", conn_low, table, preferred_element_type=jnp.float32
        )
        inputs = (rate.astype(jnp.float32) + drive).astype(jnp.bfloat16)
        mixed = jnp.dot(
            inputs.reshape(-1, width), w_local, preferred_element_type=jnp.float32
        ).reshape(current.shape)
        current = (
            (1.0 - RELAX_RATE) * current
            + RELAX_RATE * mixed
            + noise[step_index].astype(jnp.float32)
        )
    picked_obs = jnp.take(current, observed[0], axis=1)
    image_local = jnp.einsum("mos,s->mo", picked_obs, readout, precision=lax.Precision.HIGHEST)
    innov_local = (
        obs_value[0][None, :] + jnp.sqrt(obs_var[0])[None, :] * obs_pert[:, 0, :] - image_local
    )
    image_all, innov_all = (
        lax.all_gather(image_local, "member", axis=0, tiled=True),
        lax.all_gather(innov_local, "member", axis=0, tiled=True),
    )
    members_count = image_all.shape[0]
    anomaly = image_all - jnp.mean(image_all, axis=0, keepdims=True)
    covar = jnp.dot(anomaly.T, anomaly, precision=lax.Precision.HIGHEST) / (
        members_count - 1
    ) + jnp.diag(obs_var[0])
    factor = jnp.linalg.cholesky(covar)
    gain = jax.scipy.linalg.cho_solve((factor, True), innov_all.T).T
    mixing = jnp.dot(gain, anomaly.T, precision=lax.Precision.HIGHEST) / (members_count - 1)
    mixing = mixing - jnp.mean(mixing, axis=1, keepdims=True)
    member_index = lax.axis_index("member")
    flat = current.reshape(mem_local, vox_local * width)
    mine_rows = lax.dynamic_slice_in_dim(mixing, member_index * mem_local, mem_local, 0)
    result = flat + jnp.dot(
        mine_rows,
        lax.all_gather(flat.astype(jnp.bfloat16), "member", axis=0, tiled=True).astype(jnp.float32),
        precision=lax.Precision.HIGHEST,
    )
    return result.reshape(mem_local, vox_local, width)


def solution(mesh):
    in_specs = (
        P("member", "dom", None),
        P(None, "member", "dom", None),
        P(),
        P(None, "dom"),
        P(None, "dom"),
        P("dom", None),
        P(),
        P(),
        P("dom", None),
        P("dom", None),
        P("dom", None),
        P("member", "dom", None),
    )
    out_specs = P("member", "dom", None)
    return jax.shard_map(
        per_device, mesh=mesh, in_specs=in_specs, out_specs=out_specs, check_vma=False
    )
```

profile of v0, /device:TPU:0, one launch (start us, length us, event | category | flops | bytes accessed | tf_op | source)
XLA Modules:
  0.0 218.6 jit_solution(7088753334760143490)
XLA Ops:
  6.5 0.7 constant_dynamic-slice_fusion
  7.5 1.4 gather_fusion.1
  8.9 1.6 tanh_convert_fusion.7
  10.5 0.4 copy.81
  11.0 0.6 gather_fusion.2
  11.5 0.8 select_bitcast_fusion.7
  12.4 7.3 %all-to-all-start = ((bf16[8,32,512]{2,0,1:T(8,128)(2,1)}), bf16[8,32,512]{2,0,1:T(8,128)(2,1)S(1)}, u32[]{:S(2)}, u32[]{:S(2)}) async-start(bf16[8,32,512]{2,0,1:T(8,128)(2,1)} %select_bitcast_fusion.7), calls=%async_computation | async-start | bytes 524288 | tf_op jit(solution)/shard_map/all_to_all | solution.py:38
  19.7 0.6 select_reduce_fusion
  20.3 8.3 %all-to-all-done = bf16[8,32,512]{2,0,1:T(8,128)(2,1)S(1)} async-done(((bf16[8,32,512]{2,0,1:T(8,128)(2,1)}), bf16[8,32,512]{2,0,1:T(8,128)(2,1)S(1)}, u32[]{:S(2)}, u32[]{:S(2)}) %all-to-all-start) | async-done | bytes 262176 | tf_op jit(solution)/shard_map/all_to_all | solution.py:38
  28.6 1.5 fusion.8
  30.1 4.2 %tanh_convert_fusion.6 = (bf16[8,96,512]{2,1,0:T(8,128)(2,1)S(1)}, f32[8,96,512]{2,1,0:T(8,128)}) fusion(bf16[8,8,96,512]{3,2,1,0:T(8,128)(2,1)} %param.17, f32[8,96,512]{2,1,0:T(8,128)} %param.16, bf16[512,512]{1,0:T(8,128)(2,1)S(1)} %copy-done, f32[8,512,96]{1,2,0:T(8,128)} %fusion.8, bf16[8,96,512]{2,1,0:T(8,128)(2,1)S(1)} %tanh_convert_fusion.7, ...), kind=kOutput, calls=%fused_computation.41 | convolution fusion | flops 508952576 | bytes 8675328 | tf_op jit(solution)/shard_map/dot_general | solution.py:45
  34.3 0.4 copy.83
  34.8 0.7 gather_fusion.3
  35.5 0.1 select_bitcast_fusion.6
  35.6 12.0 %all_to_all.40 = bf16[8,32,512]{2,0,1:T(8,128)(2,1)S(1)} all-to-all(bf16[8,32,512]{2,0,1:T(8,128)(2,1)S(1)} %select_bitcast_fusion.6), channel_id=1, replica_groups=mesh['dom'=8,'member'=4] {'dom'}, dimensions={1} | all-to-all | bytes 524288 | tf_op jit(solution)/shard_map/all_to_all | solution.py:38
  47.6 1.5 fusion.9
  49.1 4.2 %tanh_convert_fusion.5 = (bf16[8,96,512]{2,1,0:T(8,128)(2,1)S(1)}, f32[8,96,512]{2,1,0:T(8,128)}) fusion(bf16[8,8,96,512]{3,2,1,0:T(8,128)(2,1)} %param.17, f32[8,96,512]{2,1,0:T(8,128)} %get-tuple-element.12, bf16[512,512]{1,0:T(8,128)(2,1)S(1)} %copy-done, f32[8,512,96]{1,2,0:T(8,128)} %fusion.9, bf16[8,96,512]{2,1,0:T(8,128)(2,1)S(1)} %get-tuple-element.11, ...), kind=kOutput, calls=%fused_computation.40 | convolution fusion | flops 508952576 | bytes 8675328 | tf_op jit(solution)/shard_map/dot_general | solution.py:45
  53.3 0.4 copy.85
  53.7 0.7 gather_fusion.4
  54.5 11.9 %all_to_all.41 = bf16[8,32,512]{2,0,1:T(8,128)(2,1)S(1)} all-to-all(bf16[8,32,512]{2,0,1:T(8,128)(2,1)S(1)} %select_bitcast_fusion.5), channel_id=1, replica_groups=mesh['dom'=8,'member'=4] {'dom'}, dimensions={1} | all-to-all | bytes 524288 | tf_op jit(solution)/shard_map/all_to_all | solution.py:38
  66.5 1.5 fusion.10
  68.0 4.2 %tanh_convert_fusion.4 = (bf16[8,96,512]{2,1,0:T(8,128)(2,1)S(1)}, f32[8,96,512]{2,1,0:T(8,128)}) fusion(bf16[8,8,96,512]{3,2,1,0:T(8,128)(2,1)} %param.17, f32[8,96,512]{2,1,0:T(8,128)} %get-tuple-element.14, bf16[512,512]{1,0:T(8,128)(2,1)S(1)} %copy-done, f32[8,512,96]{1,2,0:T(8,128)} %fusion.10, bf16[8,96,512]{2,1,0:T(8,128)(2,1)S(1)} %get-tuple-element.13, ...), kind=kOutput, calls=%fused_computation.39 | convolution fusion | flops 508952576 | bytes 8675328 | tf_op jit(solution)/shard_map/dot_general | solution.py:45
  72.2 0.4 copy.87
  72.6 0.7 gather_fusion.5
  73.5 11.8 %all_to_all.42 = bf16[8,32,512]{2,0,1:T(8,128)(2,1)S(1)} all-to-all(bf16[8,32,512]{2,0,1:T(8,128)(2,1)S(1)} %select_bitcast_fusion.4), channel_id=1, replica_groups=mesh['dom'=8,'member'=4] {'dom'}, dimensions={1} | all-to-all | bytes 524288 | tf_op jit(solution)/shard_map/all_to_all | solution.py:38
  85.4 1.5 fusion.11
  86.9 4.2 %tanh_convert_fusion.3 = (bf16[8,96,512]{2,1,0:T(8,128)(2,1)S(1)}, f32[8,96,512]{2,1,0:T(8,128)}) fusion(bf16[8,8,96,512]{3,2,1,0:T(8,128)(2,1)} %param.17, f32[8,96,512]{2,1,0:T(8,128)} %get-tuple-element.16, bf16[512,512]{1,0:T(8,128)(2,1)S(1)} %copy-done, f32[8,512,96]{1,2,0:T(8,128)} %fusion.11, bf16[8,96,512]{2,1,0:T(8,128)(2,1)S(1)} %get-tuple-element.15, ...), kind=kOutput, calls=%fused_computation.38 | convolution fusion | flops 508952576 | bytes 8675328 | tf_op jit(solution)/shard_map/dot_general | solution.py:45
  91.0 0.4 copy.89
  91.5 0.7 gather_fusion.6
  92.3 11.8 %all_to_all.43 = bf16[8,32,512]{2,0,1:T(8,128)(2,1)S(1)} all-to-all(bf16[8,32,512]{2,0,1:T(8,128)(2,1)S(1)} %select_bitcast_fusion.3), channel_id=1, replica_groups=mesh['dom'=8,'member'=4] {'dom'}, dimensions={1} | all-to-all | bytes 524288 | tf_op jit(solution)/shard_map/all_to_all | solution.py:38
  104.2 1.5 fusion.12
  105.7 4.2 %tanh_convert_fusion.2 = (bf16[8,96,512]{2,1,0:T(8,128)(2,1)S(1)}, f32[8,96,512]{2,1,0:T(8,128)}) fusion(bf16[8,8,96,512]{3,2,1,0:T(8,128)(2,1)} %param.17, f32[8,96,512]{2,1,0:T(8,128)} %get-tuple-element.18, bf16[512,512]{1,0:T(8,128)(2,1)S(1)} %copy-done, f32[8,512,96]{1,2,0:T(8,128)} %fusion.12, bf16[8,96,512]{2,1,0:T(8,128)(2,1)S(1)} %get-tuple-element.17, ...), kind=kOutput, calls=%fused_computation.37 | convolution fusion | flops 508952576 | bytes 8675328 | tf_op jit(solution)/shard_map/dot_general | solution.py:45
  109.9 0.4 copy.91
  110.3 0.7 gather_fusion.7
  111.1 11.8 %all_to_all.44 = bf16[8,32,512]{2,0,1:T(8,128)(2,1)S(1)} all-to-all(bf16[8,32,512]{2,0,1:T(8,128)(2,1)S(1)} %select_bitcast_fusion.2), channel_id=1, replica_groups=mesh['dom'=8,'member'=4] {'dom'}, dimensions={1} | all-to-all | bytes 524288 | tf_op jit(solution)/shard_map/all_to_all | solution.py:38
  123.0 1.5 fusion.13
  124.5 4.2 %tanh_convert_fusion.1 = (bf16[8,96,512]{2,1,0:T(8,128)(2,1)S(1)}, f32[8,96,512]{2,1,0:T(8,128)}) fusion(bf16[8,8,96,512]{3,2,1,0:T(8,128)(2,1)} %param.17, f32[8,96,512]{2,1,0:T(8,128)} %get-tuple-element.20, bf16[512,512]{1,0:T(8,128)(2,1)S(1)} %copy-done, f32[8,512,96]{1,2,0:T(8,128)} %fusion.13, bf16[8,96,512]{2,1,0:T(8,128)(2,1)S(1)} %get-tuple-element.19, ...), kind=kOutput, calls=%fused_computation.36 | convolution fusion | flops 508952576 | bytes 8675328 | tf_op jit(solution)/shard_map/dot_general | solution.py:45
  128.7 0.4 copy.93
  129.1 0.7 gather_fusion.8
  129.9 11.8 %all_to_all.45 = bf16[8,32,512]{2,0,1:T(8,128)(2,1)S(1)} all-to-all(bf16[8,32,512]{2,0,1:T(8,128)(2,1)S(1)} %select_bitcast_fusion.1), channel_id=1, replica_groups=mesh['dom'=8,'member'=4] {'dom'}, dimensions={1} | all-to-all | bytes 524288 | tf_op jit(solution)/shard_map/all_to_all | solution.py:38
  141.8 1.5 fusion.14
  143.3 4.2 %tanh_convert_fusion = (bf16[8,96,512]{2,1,0:T(8,128)(2,1)S(1)}, f32[8,96,512]{2,1,0:T(8,128)}) fusion(bf16[8,8,96,512]{3,2,1,0:T(8,128)(2,1)} %param.17, f32[8,96,512]{2,1,0:T(8,128)} %get-tuple-element.22, bf16[512,512]{1,0:T(8,128)(2,1)S(1)} %copy-done, f32[8,512,96]{1,2,0:T(8,128)} %fusion.14, bf16[8,96,512]{2,1,0:T(8,128)(2,1)S(1)} %get-tuple-element.21, ...), kind=kOutput, calls=%fused_computation.35 | convolution fusion | flops 508952576 | bytes 8675328 | tf_op jit(solution)/shard_map/dot_general | solution.py:45
  147.5 0.4 copy.95
  148.0 0.7 gather_fusion.9
  148.8 11.8 %all_to_all.46 = bf16[8,32,512]{2,0,1:T(8,128)(2,1)S(1)} all-to-all(bf16[8,32,512]{2,0,1:T(8,128)(2,1)S(1)} %select_bitcast_fusion), channel_id=1, replica_groups=mesh['dom'=8,'member'=4] {'dom'}, dimensions={1} | all-to-all | bytes 524288 | tf_op jit(solution)/shard_map/all_to_all | solution.py:38
  160.7 1.5 fusion.15
  162.2 4.1 %convert_add_fusion = f32[8,96,512]{2,1,0:T(8,128)} fusion(f32[8,96,512]{2,1,0:T(8,128)} %get-tuple-element.24, f32[8,512,96]{1,2,0:T(8,128)} %fusion.15, bf16[8,96,512]{2,1,0:T(8,128)(2,1)S(1)} %get-tuple-element.23, bf16[96,128,1]{1,0,2:T(8,128)(2,1)S(1)} %get-tuple-element.6, bf16[8,32,512]{2,1,0:T(8,128)(2,1)S(1)} %copy.96, ...), kind=kOutput, calls=%fused_computation.11 | convolution fusion | flops 508559360 | bytes 7888896 | tf_op jit(solution)/shard_map/dot_general | solution.py:45
  166.2 2.3 %copy.103 = f32[1,8,96,512]{3,1,2,0:T(8,128)S(1)} copy(f32[1,8,96,512]{3,2,1,0:T(8,128)} %bitcast.202) | data formatting | bytes 3145728
  168.6 1.0 convert_element_type.176
  169.7 3.5 %copy.97 = f32[8,96,512]{2,0,1:T(8,128)} copy(f32[8,96,512]{2,1,0:T(8,128)} %convert_add_fusion) | data formatting | bytes 3145728 | tf_op jit(solution)/shard_map/add | solution.py:49
  173.2 2.1 gather_fusion
  175.3 7.1 %fusion.16 = f32[1,8,64]{1,0,2:T(1,128)S(1)} fusion(f32[512,1,1]{0,1,2:T(1,128)S(1)} %bitcast.206, f32[64,8,512]{2,1,0:T(8,128)S(1)} %gather_fusion, pred[64]{0:T(512)(128)(4,1)S(1)} %compare_and_fusion.1), kind=kOutput, calls=%fused_computation.61 | convolution fusion | flops 3407872 | bytes 1052736 | tf_op jit(solution)/shard_map/mos,s->mo/dot_general | solution.py:54
  182.4 5.4 %all_gather.9 = f32[32,64]{1,0:T(8,128)S(1)} all-gather(f32[8,64]{1,0:T(8,128)S(1)} %bitcast.204), channel_id=1, replica_groups=mesh['dom'=8,'member'=4] {'member'}, dimensions={0}, use_global_device_ids=true | all-gather | bytes 10240 | tf_op jit(solution)/shard_map/all_gather | solution.py:59
  187.9 0.2 convolution_multiply_fusion
  188.3 5.9 %cholesky.16 = f32[64,64]{1,0:T(8,128)S(1)} custom-call(f32[64,64]{1,0:T(8,128)S(1)} %fusion.35), custom_call_target="Cholesky" | custom-call | tf_op jit(solution)/shard_map/jit(cholesky)/cholesky | solution.py:67
  194.2 0.6 compare_reduce_fusion
  194.8 0.7 fusion.29
  195.5 4.9 %custom-call.10 = f32[1,64,64]{1,2,0:T(8,128)S(1)} custom-call(f32[1,64,64]{2,1,0:T(8,128)S(1)} %fusion.29), custom_call_target="InvertDiagBlocksLowerTriangular" | custom-call | tf_op jit(solution)/shard_map/jit(_cho_solve)/triangular_solve | solution.py:68
  200.4 5.2 %all_gather.10 = f32[32,64]{1,0:T(8,128)S(1)} all-gather(f32[8,64]{1,0:T(8,128)S(1)} %add_subtract_fusion), channel_id=1, replica_groups=mesh['dom'=8,'member'=4] {'member'}, dimensions={0}, use_global_device_ids=true | all-gather | bytes 10240 | tf_op jit(solution)/shard_map/all_gather | solution.py:60
  205.6 0.1 fusion.32
  205.8 0.2 fusion.30
  205.9 0.3 fusion.77
  206.3 3.4 %convolution_add_fusion = f32[8,49152]{1,0:T(8,128)S(1)} fusion(f32[8,49152]{1,0:T(8,128)S(1)} %bitcast.201, bf16[32,49152]{1,0:T(8,128)(2,1)} %all-gather.2.cloned.1.call-done, f32[32,32]{1,0:T(8,128)S(1)} %get-tuple-element.26, s32[]{:T(128)S(6)} %select_n.64, f32[8]{0:T(128)S(1)} %dynamic-slice), kind=kOutput, calls=%fused_computation.10 | convolution fusion | flops 151388416 | bytes 6296068 | tf_op jit(solution)/shard_map/dot_general | solution.py:74
  209.7 2.1 copy.100
  (55 shorter events, 2.0 us)
Async XLA Ops:
  6.5 23.6 %copy-start = (bf16[512,512]{1,0:T(8,128)(2,1)S(1)}, bf16[512,512]{1,0:T(8,128)(2,1)}, u32[]{:S(2)}) copy-start(bf16[512,512]{1,0:T(8,128)(2,1)} %param.18) | copy-start | bytes 1572868
  8.9 2.1 copy-start.1
  10.5 9.2 %copy-start.2 = (f32[16,96]{1,0:T(8,128)S(1)}, f32[16,96]{1,0:T(8,128)}, u32[]{:S(2)}) copy-start(f32[16,96]{1,0:T(8,128)} %param.19) | copy-start | bytes 18436
  10.5 9.2 %copy-start.3 = (s32[16,96]{1,0:T(8,128)S(1)}, s32[16,96]{1,0:T(8,128)}, u32[]{:S(2)}) copy-start(s32[16,96]{1,0:T(8,128)} %param.20) | copy-start | bytes 18436
  12.4 16.2 %all-to-all-start = ((bf16[8,32,512]{2,0,1:T(8,128)(2,1)}), bf16[8,32,512]{2,0,1:T(8,128)(2,1)S(1)}, u32[]{:S(2)}, u32[]{:S(2)}) async-start(bf16[8,32,512]{2,0,1:T(8,128)(2,1)} %select_bitcast_fusion.7), calls=%async_computation | async-start | bytes 524288 | tf_op jit(solution)/shard_map/all_to_all | solution.py:38
  19.6 186.7 %all-gather.2.cloned.1.call-start = ((), (), s32[]{:S(2)}) async-start(), calls=%async_computation.8 | async-start | bytes 3932160 | tf_op jit(solution)/shard_map/all_gather | solution.py:76
  168.6 1.1 copy-start.8
  168.6 1.1 copy-start.6
  173.1 2.1 copy-start.5
  173.1 27.3 %copy-start.4 = (f32[8,1,64]{2,1,0:T(1,128)S(1)}, f32[8,1,64]{2,1,0:T(1,128)}, u32[]{:S(2)}) copy-start(f32[8,1,64]{2,1,0:T(1,128)} %param.27) | copy-start | bytes 6148
  173.2 27.3 %copy-start.7 = (f32[1,64]{1,0:T(1,128)S(1)}, f32[1,64]{1,0:T(1,128)}, u32[]{:S(2)}) copy-start(f32[1,64]{1,0:T(1,128)} %param.25) | copy-start | bytes 772
Sparse Core Ops, SparseCore 0:
  169.7 27.6 all-gather.1
where the time goes:
time: 219 us
  blocking collectives  93.6 us (43%)
  matrix products  56.6 us (26%)
  local copies, waits for them, and re-layouts  22 us (10%)
  other arithmetic  17 us (8%)
  between operations  13.8 us (6%)
  waiting for transfers between devices  8.29 us (4%)
  starting transfers between devices  7.32 us (3%)
    all_to_all x7, blocking collectives, per_device(): lax.all_to_all(outgoing, 'dom', split_axis=1, concat_axis=1, tiled=True)  82.9 us
    dot_general x8, matrix products, per_device(): jnp.dot(inputs.reshape(-1, width), w_local, preferred_element_type=jnp.fl...  33.3 us
    dot_general x8, matrix products, per_device(): jnp.einsum('vu,mus->mvs', conn_high, table, preferred_element_type=jnp.fl...  12 us
    all_to_all x1, waiting for transfers between devices, per_device(): lax.all_to_all(outgoing, 'dom', split_axis=1, concat_axis=1, tiled=True)  8.27 us
    all_to_all x1, starting transfers between devices, per_device(): lax.all_to_all(outgoing, 'dom', split_axis=1, concat_axis=1, tiled=True)  7.28 us
    dot_general x1, matrix products, per_device(): jnp.einsum('mos,s->mo', picked_obs, readout, precision=lax.Precision.HIGH...  7.06 us
    another operation x3, other arithmetic, per_device(): factor = jnp.linalg.cholesky(covar)  6.52 us
    another operation x2, other arithmetic, per_device(): gain = jax.scipy.linalg.cho_solve((factor, True), innov_all.T).T  5.55 us
  transfers between devices with their start and end apart: 2, of which 1 were waited for; matrix products, arithmetic and copies ran while one was open for 12% of the time, Pallas kernels for 0%

commit v1 on v0

v1 whole, which is shorter than its diff:
```python
import functools

import jax
import jax.numpy as jnp
from jax import lax
from jax.experimental import pallas as pl
from jax.experimental.pallas import tpu as pltpu
from jax.sharding import PartitionSpec as P

MESH = pl.DeviceIdType.MESH
HIGHEST = lax.Precision.HIGHEST
F32 = jnp.float32
BF16 = jnp.bfloat16


def kernel(
    n,
    nm,
    group,
    cap,
    chunk,
    state_hbm,
    noise_hbm,
    w_ref,
    conn_ref,
    sel_ref,
    readout_ref,
    observed_ref,
    value_ref,
    var_ref,
    pert_ref,
    out_hbm,
    cur,
    noise,
    rate,
    sendbuf,
    recvbuf,
    ens,
    images,
    padded,
    state_sem,
    noise_sem,
    send_sem,
    recv_sem,
    ens_send,
    ens_recv,
    fwd_send,
    img_send,
    img_recv,
    out_sem,
):
    members, vox, width = cur.shape
    steps = noise.shape[0]
    groups = members // group
    block = group * cap
    me = lax.axis_index("dom")
    mi = lax.axis_index("member")
    sib = mi + 1 - 2 * lax.rem(mi, 2)
    chunks = vox // chunk

    def dom_peer(d):
        return lax.rem(me + d, n)

    def mem_peer(d):
        return lax.rem(mi + d, nm)

    def state_copy(g):
        rows = pl.ds(g * group, group)
        return pltpu.make_async_copy(state_hbm.at[rows], cur.at[rows], state_sem.at[g])

    def noise_copy(k):
        return pltpu.make_async_copy(noise_hbm.at[k], noise.at[k], noise_sem.at[k])

    for g in range(groups):
        state_copy(g).start()
    for k in range(steps):
        noise_copy(k).start()

    barrier = pltpu.get_barrier_semaphore()
    for d in range(1, n):
        pl.semaphore_signal(barrier, inc=1, device_id=(dom_peer(d), mi), device_id_type=MESH)
    for d in range(1, nm):
        pl.semaphore_signal(barrier, inc=1, device_id=(me, mem_peer(d)), device_id_type=MESH)

    def halo_copy(g, slot, d):
        return pltpu.make_async_remote_copy(
            src_ref=sendbuf.at[g, slot, dom_peer(d)],
            dst_ref=recvbuf.at[g, slot, me],
            send_sem=send_sem.at[g, slot, d],
            recv_sem=recv_sem.at[g, slot, d],
            device_id=(dom_peer(d), mi),
            device_id_type=MESH,
        )

    def halo_arrival(g, slot, d):
        source = lax.rem(me + n - d, n)
        return pltpu.make_async_remote_copy(
            src_ref=sendbuf.at[g, slot, source],
            dst_ref=recvbuf.at[g, slot, source],
            send_sem=send_sem.at[g, slot, d],
            recv_sem=recv_sem.at[g, slot, d],
            device_id=(source, mi),
            device_id_type=MESH,
        )

    order = sorted(range(1, n), key=lambda d: abs(2 * d - n))

    def make_rate(g):
        rows = pl.ds(g * group, group)
        rate[rows] = jnp.tanh(cur[rows]).astype(BF16)

    def send(g, slot):
        rows = pl.ds(g * group, group)
        picked = jnp.dot(
            sel_ref[...], rate[rows].reshape(group * vox, width), preferred_element_type=F32
        )
        sendbuf[g, slot] = picked.astype(BF16).reshape(n, block, width)
        for d in order:
            halo_copy(g, slot, d).start()
        recvbuf[g, slot, me] = sendbuf[g, slot, me]

    def receive(g, slot):
        for d in order:
            halo_arrival(g, slot, d).wait_recv()
        for d in order:
            halo_copy(g, slot, d).wait_send()

    def update(g, slot, k):
        halo = recvbuf[g, slot].reshape(n * block, width)
        for m in range(group):
            i = g * group + m
            table = jnp.concatenate([halo, rate[i]], axis=0)
            inputs = jnp.dot(conn_ref[m], table, preferred_element_type=F32).astype(BF16)
            mixed = jnp.dot(inputs, w_ref[...], preferred_element_type=F32)
            cur[i] = 0.5 * (cur[i] + mixed) + noise[k, i].astype(F32)

    for g in range(groups):
        state_copy(g).wait()
        make_rate(g)
        if g == 0:
            pl.semaphore_wait(barrier, n - 1 + nm - 1)
        send(g, 0)

    def step(k, carry):
        slot = lax.rem(k, 2)
        noise_copy(k).wait()
        for g in range(groups):
            receive(g, slot)
            update(g, slot, k)
            make_rate(g)
            send(g, 1 - slot)
        return carry

    lax.fori_loop(0, steps - 1, step, 0)

    def ens_piece(dev, g, c):
        return ens.at[dev, g, :, pl.ds(c * chunk, chunk)]

    def ens_copy(dev, g, c, target, send_to, recv_to):
        return pltpu.make_async_remote_copy(
            src_ref=ens_piece(dev, g, c),
            dst_ref=ens_piece(dev, g, c),
            send_sem=send_to,
            recv_sem=recv_to,
            device_id=(me, target),
            device_id_type=MESH,
        )

    far = range(2, nm, 2)

    def own_copy(g, c, d):
        target = sib if d == 0 else mem_peer(d)
        return ens_copy(mi, g, c, target, ens_send.at[g, c, d // 2], ens_recv.at[g, c, d // 2])

    def own_arrival(g, c, d):
        source = sib if d == 0 else lax.rem(mi + nm - d, nm)
        return ens_copy(source, g, c, source, ens_send.at[g, c, d // 2], ens_recv.at[g, c, d // 2])

    def forward_copy(g, c, d):
        source = lax.rem(mi + nm - d, nm)
        return ens_copy(
            source, g, c, sib, fwd_send.at[g, c, d // 2], ens_recv.at[g, c, nm // 2 + d // 2]
        )

    def forward_arrival(g, c, d):
        source = lax.rem(sib + nm - d, nm)
        return ens_copy(
            source, g, c, sib, fwd_send.at[g, c, d // 2], ens_recv.at[g, c, nm // 2 + d // 2]
        )

    obs = observed_ref.shape[1]
    padded[...] = jnp.zeros_like(padded)
    padded[0:1, 0:obs] = value_ref[...]
    padded[1:2, :] = jnp.ones((1, padded.shape[1]), F32)
    padded[1:2, 0:obs] = var_ref[...]
    padded[2:3, 0:obs] = observed_ref[...].astype(F32) + 1.0
    padded[8 : 8 + members, 0:obs] = pert_ref[:, 0, :]
    lanes = padded.shape[1]
    vox_iota = lax.broadcasted_iota(jnp.int32, (vox, lanes), 0).astype(F32) + 1.0
    pick = jnp.where(vox_iota == padded[2:3, :], 1.0, 0.0)

    last = steps - 1
    slot = last % 2
    noise_copy(last).wait()
    for g in range(groups):
        receive(g, slot)
        update(g, slot, last)
        rows = pl.ds(g * group, group)
        ens[mi, g] = cur[rows].astype(BF16)
        for c in range(chunks):
            for d in far:
                own_copy(g, c, d).start()
        for c in range(chunks):
            own_copy(g, c, 0).start()
        for m in range(group):
            seen = jnp.sum(cur[g * group + m] * readout_ref[...], axis=1, keepdims=True)
            images[mi, g * group + m, :] = jnp.sum(pick * seen, axis=0)

    def img_copy(d):
        return pltpu.make_async_remote_copy(
            src_ref=images.at[mi],
            dst_ref=images.at[mi],
            send_sem=img_send.at[d],
            recv_sem=img_recv.at[d],
            device_id=(me, mem_peer(d)),
            device_id_type=MESH,
        )

    def img_arrival(d):
        source = lax.rem(mi + nm - d, nm)
        return pltpu.make_async_remote_copy(
            src_ref=images.at[source],
            dst_ref=images.at[source],
            send_sem=img_send.at[d],
            recv_sem=img_recv.at[d],
            device_id=(me, source),
            device_id_type=MESH,
        )

    for d in range(1, nm):
        img_copy(d).start()
    for d in range(1, nm):
        img_arrival(d).wait_recv()

    total = nm * members
    var = padded[1:2, :]
    innov = padded[0:1, :] + jnp.sqrt(var) * padded[8 : 8 + members, :] - images[mi]
    image_all = images[...].reshape(total, lanes)
    anomaly = image_all - jnp.mean(image_all, axis=0, keepdims=True)
    scaled = anomaly / (var * (total - 1))
    nt = (((1,), (1,)), ((), ()))
    system = lax.dot_general(
        scaled,
        jnp.concatenate([anomaly, innov], axis=0),
        nt,
        precision=HIGHEST,
        preferred_element_type=F32,
    )
    row_id = lax.broadcasted_iota(jnp.int32, system.shape, 0)
    col_id = lax.broadcasted_iota(jnp.int32, system.shape, 1)
    system = system + jnp.where(row_id == col_id, 1.0, 0.0)
    column_rows = lax.broadcasted_iota(jnp.int32, (total, 1), 0)
    for j in range(total):
        row = system[j : j + 1, :] / system[j : j + 1, j : j + 1]
        column = system[:, j : j + 1] - jnp.where(column_rows == j, 1.0, 0.0)
        system = system - column * row
    mix = system[:, total : total + members]
    mix = mix - jnp.mean(mix, axis=0, keepdims=True)

    sub = 16
    e1 = jnp.where(
        lax.broadcasted_iota(jnp.int32, (members * sub, members), 0) // sub
        == lax.broadcasted_iota(jnp.int32, (members * sub, members), 1),
        1.0,
        0.0,
    )
    e2 = jnp.where(
        lax.broadcasted_iota(jnp.int32, (total, total * sub), 1) // sub
        == lax.broadcasted_iota(jnp.int32, (total, total * sub), 0),
        1.0,
        0.0,
    )
    wide = lax.dot_general(e1, mix, nt, precision=HIGHEST, preferred_element_type=F32)
    wide = jnp.dot(wide, e2, precision=HIGHEST, preferred_element_type=F32)
    same = lax.rem(lax.broadcasted_iota(jnp.int32, wide.shape, 0), sub) == lax.rem(
        lax.broadcasted_iota(jnp.int32, wide.shape, 1), sub
    )
    wide = jnp.where(same, wide, 0.0)
    high = wide.astype(BF16)
    low = (wide - high.astype(F32)).astype(BF16)
    both = jnp.concatenate([high, low], axis=0)

    for g in range(groups - 1):
        for c in range(chunks):
            for d in far:
                own_arrival(g, c, d).wait_recv()
                forward_copy(g, c, d).start()
    for c in range(chunks):
        g = groups - 1
        for d in far:
            own_arrival(g, c, d).wait_recv()
            forward_copy(g, c, d).start()
        for g in range(groups):
            own_arrival(g, c, 0).wait_recv()
            for d in far:
                forward_arrival(g, c, d).wait_recv()
        for s in range(chunk // sub):
            rows = pl.ds(c * chunk + s * sub, sub)
            data = ens[:, :, :, rows].reshape(total * sub, width)
            added = jnp.dot(both, data, preferred_element_type=F32)
            half = members * sub
            added = (added[:half] + added[half:]).reshape(members, sub, width)
            cur[:, rows] = cur[:, rows] + added
        piece = pl.ds(c * chunk, chunk)
        pltpu.make_async_copy(cur.at[:, piece], out_hbm.at[:, piece], out_sem.at[c]).start()

    for c in range(chunks):
        piece = pl.ds(c * chunk, chunk)
        pltpu.make_async_copy(cur.at[:, piece], out_hbm.at[:, piece], out_sem.at[c]).wait()
        for g in range(groups):
            own_copy(g, c, 0).wait_send()
            for d in far:
                own_copy(g, c, d).wait_send()
                forward_copy(g, c, d).wait_send()
    for d in range(1, nm):
        img_copy(d).wait_send()


def per_device(
    state,
    noise,
    w_local,
    conn_weight,
    conn_index,
    boundary,
    send_pos,
    readout,
    observed,
    obs_value,
    obs_var,
    obs_pert,
):
    members, vox, width = state.shape
    steps = noise.shape[0]
    n = lax.axis_size("dom")
    nm = lax.axis_size("member")
    me = lax.axis_index("dom")
    cap = send_pos.shape[2]
    obs = observed.shape[1]
    group = max(1, min(members, 16 // cap))
    groups = members // group
    block = group * cap
    chunk = 32

    halo = conn_index - vox
    slots = (halo // cap) * block + lax.rem(halo, cap)
    column = jnp.arange(n * block + vox, dtype=jnp.int32)
    member = jnp.arange(group, dtype=jnp.int32)
    target = jnp.where(
        (halo < 0)[:, None, :],
        (conn_index + n * block)[:, None, :],
        slots[:, None, :] + member[None, :, None] * cap,
    )
    conn = jnp.sum(
        jnp.where(target[..., None] == column, conn_weight[:, None, :, None], 0.0), axis=0
    )
    own = (column[None, :] - n * block) == jnp.arange(vox, dtype=jnp.int32)[:, None]
    conn = (conn + own[None].astype(F32)).astype(BF16)

    mine = lax.dynamic_index_in_dim(send_pos, me, 0, keepdims=False)
    which = jnp.arange(boundary.shape[1], dtype=jnp.int32)
    local = jnp.sum(jnp.where(mine[..., None] == which, boundary[0], 0), axis=-1)
    flat = jnp.arange(group * vox, dtype=jnp.int32)
    sel = flat == local[:, None, :, None] + member[None, :, None, None] * vox
    sel = sel.astype(BF16).reshape(n * block, group * vox)

    vmem = pl.BlockSpec(memory_space=pltpu.VMEM)
    anywhere = pl.BlockSpec(memory_space=pl.ANY)
    dma = pltpu.SemaphoreType.DMA
    chunks = vox // chunk
    lanes = -(-obs // 128) * 128
    return pl.pallas_call(
        functools.partial(kernel, n, nm, group, cap, chunk),
        out_shape=jax.ShapeDtypeStruct(state.shape, F32),
        in_specs=[anywhere, anywhere] + [vmem] * 8,
        out_specs=anywhere,
        scratch_shapes=[
            pltpu.VMEM((members, vox, width), F32),
            pltpu.VMEM((steps, members, vox, width), BF16),
            pltpu.VMEM((members, vox, width), BF16),
            pltpu.VMEM((groups, 2, n, block, width), BF16),
            pltpu.VMEM((groups, 2, n, block, width), BF16),
            pltpu.VMEM((nm, groups, group, vox, width), BF16),
            pltpu.VMEM((nm, members, lanes), F32),
            pltpu.VMEM((8 + members, lanes), F32),
            dma((groups,)),
            dma((steps,)),
            dma((groups, 2, n)),
            dma((groups, 2, n)),
            dma((groups, chunks, nm)),
            dma((groups, chunks, nm)),
            dma((groups, chunks, nm)),
            dma((nm,)),
            dma((nm,)),
            dma((chunks,)),
        ],
        compiler_params=pltpu.CompilerParams(
            collective_id=0, has_side_effects=True, vmem_limit_bytes=48 * 1024 * 1024
        ),
    )(
        state,
        noise,
        w_local,
        conn,
        sel,
        readout[None, :],
        observed,
        obs_value,
        obs_var,
        obs_pert,
    )


def solution(mesh):
    in_specs = (
        P("member", "dom", None),
        P(None, "member", "dom", None),
        P(),
        P(None, "dom"),
        P(None, "dom"),
        P("dom", None),
        P(),
        P(),
        P("dom", None),
        P("dom", None),
        P("dom", None),
        P("member", "dom", None),
    )
    return jax.shard_map(
        per_device,
        mesh=mesh,
        in_specs=in_specs,
        out_specs=P("member", "dom", None),
        check_vma=False,
    )
```

time: 219 us -> 95.1 us (0.43)
  blocking collectives: 93.6 us -> 0 us
  Pallas kernels: 0 us -> 82.1 us
  matrix products: 56.6 us -> 0 us
  local copies, waits for them, and re-layouts: 22 us -> 7.82 us
  between operations: 13.8 us -> 0.06 us
  other arithmetic: 17 us -> 4.66 us
  waiting for transfers between devices: 8.29 us -> 0 us
  starting transfers between devices: 7.32 us -> 0 us
    all_to_all x7 -> x0, blocking collectives: 82.9 us -> none  [per_device(): lax.all_to_all(outgoing, 'dom', split_axis=1, concat_axis=1, tiled=True)]
    pallas_call x0 -> x1, Pallas kernels: none -> 82.1 us  [per_device(): pl.pallas_call(functools.partial(kernel, n, nm, group, cap, chunk), out_s...]
    dot_general x20 -> x0, matrix products: 56.3 us -> none  [the longest x8 33.3 us: per_device(): jnp.dot(inputs.reshape(-1, width), w_local, preferred_element_type=jnp.fl...]
    another operation x5 -> x0, other arithmetic: 12.1 us -> none  [the longest x3 6.52 us: per_device(): factor = jnp.linalg.cholesky(covar)]
    all_gather x2 -> x0, blocking collectives: 10.6 us -> none  [the longest x1 5.45 us: per_device(): lax.all_gather(image_local, 'member', axis=0, tiled=True)]
    gather x10 -> x0, local copies, waits for them, and re-layouts: 8.88 us -> none  [the longest x8 5.41 us: per_device(): outgoing = jnp.take(rate, send_rows, axis=1)]
    all_to_all x1 -> x0, waiting for transfers between devices: 8.27 us -> none  [per_device(): lax.all_to_all(outgoing, 'dom', split_axis=1, concat_axis=1, tiled=True)]
    all_to_all x1 -> x0, starting transfers between devices: 7.28 us -> none  [per_device(): lax.all_to_all(outgoing, 'dom', split_axis=1, concat_axis=1, tiled=True)]
  transfers between devices with their start and end apart: 2 -> 0, of which waited for: 1 -> 0; matrix products, arithmetic and copies ran while one was open for 12% -> 0% of each run, Pallas kernels for 0% -> 0%
where the time goes in v1:
time: 95.1 us; the launch traced here: 94.6 us
  Pallas kernels  82.1 us (86%)
  local copies, waits for them, and re-layouts  7.82 us (8%)
  other arithmetic  4.66 us (5%)
    pallas_call x1, Pallas kernels, per_device(): pl.pallas_call(functools.partial(kernel, n, nm, group, cap, chunk), out_s...  82.1 us
    unnamed x17, local copies, waits for them, and re-layouts  7.63 us
    reduce_sum x1, other arithmetic, per_device(): jnp.sum(jnp.where(target[..., None] == column, conn_weight[:, None, :, No...  2.09 us

profile of v1, /device:TPU:0, one launch (start us, length us, event | category | flops | bytes accessed | tf_op | source)
XLA Modules:
  0.0 94.6 jit_solution(5315300395131997231)
XLA Ops:
  0.0 0.0 copy-start
  0.0 0.7 copy-done
  0.7 0.9 select_reduce_fusion.1
  1.6 0.1 copy.15
  1.7 0.7 add_compare_fusion
  2.4 0.1 broadcast_add_fusion
  2.5 0.1 add.79
  2.6 0.7 broadcast_add_fusion.1
  3.3 0.1 add_select_fusion
  3.4 0.1 fusion.sel_ref
  3.5 2.1 %select_reduce_fusion = f32[4,96,224]{2,1,0:T(8,128)S(1)} fusion(f32[16,96]{1,0:T(8,128)} %param.15, s32[16,4,96]{2,1,0:T(4,128)S(1)} %add_select_fusion), kind=kLoop, calls=%fused_computation | loop fusion | flops 4042752 | bytes 374784 | tf_op jit(solution)/shard_map/reduce_sum | solution.py:364
  5.6 0.0 copy-start.1
  5.6 1.4 %copy-done.1 = f32[8,96,512]{2,1,0:T(8,128)S(1)} copy-done((f32[8,96,512]{2,1,0:T(8,128)S(1)}, f32[8,96,512]{2,1,0:T(8,128)}, u32[]{:S(2)}) %copy-start.1) | copy-done | bytes 1572888
  7.0 0.0 copy-start.2
  7.0 1.0 %copy-done.2 = bf16[512,512]{1,0:T(8,128)(2,1)S(1)} copy-done((bf16[512,512]{1,0:T(8,128)(2,1)S(1)}, bf16[512,512]{1,0:T(8,128)(2,1)}, u32[]{:S(2)}) %copy-start.2) | copy-done | bytes 524312
  8.1 0.0 copy-start.3
  8.1 0.7 copy-done.3
  8.7 0.0 copy-start.4
  8.7 0.7 copy-done.4
  9.4 0.0 copy-start.5
  9.4 0.7 copy-done.5
  10.1 0.0 copy-start.6
  10.1 0.7 copy-done.6
  10.7 0.0 copy-start.7
  10.7 0.7 copy-done.7
  11.4 82.1 %shard_map.118 = f32[8,96,512]{2,1,0:T(8,128)S(1)} custom-call(f32[8,96,512]{2,1,0:T(8,128)S(1)} %copy-done.1, bf16[8,8,96,512]{3,2,1,0:T(8,128)(2,1)} %noise_hbm.1, bf16[512,512]{1,0:T(8,128)(2,1)S(1)} %copy-done.2, bf16[4,96,224]{2,1,0:T(8,128)(2,1)S(1)} %add_convert_fusion.conn_ref, bf16[128,384]{1,0:T(8,128)(2,1)S(1)} %fusion.sel_ref, ...), custom_call_target="tpu_custom_call" | custom-call | tf_op jit(solution)/shard_map/pallas_call | solution.py:382
  93.5 1.1 %copy.17 = f32[8,96,512]{2,1,0:T(8,128)} copy(f32[8,96,512]{2,1,0:T(8,128)S(1)} %shard_map.118) | data formatting | bytes 3145728
  (6 shorter events, 0.1 us)
Async XLA Ops:
  0.0 0.7 copy-start
  5.6 1.4 %copy-start.1 = (f32[8,96,512]{2,1,0:T(8,128)S(1)}, f32[8,96,512]{2,1,0:T(8,128)}, u32[]{:S(2)}) copy-start(f32[8,96,512]{2,1,0:T(8,128)} %state_hbm.1) | copy-start | bytes 4718596
  7.0 1.0 %copy-start.2 = (bf16[512,512]{1,0:T(8,128)(2,1)S(1)}, bf16[512,512]{1,0:T(8,128)(2,1)}, u32[]{:S(2)}) copy-start(bf16[512,512]{1,0:T(8,128)(2,1)} %w_ref.1) | copy-start | bytes 1572868
  8.1 0.7 copy-start.3
  8.7 0.7 copy-start.4
  9.4 0.7 copy-start.5
  10.1 0.7 copy-start.6
  10.7 0.7 copy-start.7

commit v2 on v1

--- a/solution.py
+++ b/solution.py
@@ -19,17 +19,35 @@
     group,
     cap,
     chunk,
+    parts,
     state_hbm,
     noise_hbm,
+    w_hbm,
+    weight_hbm,
+    index_hbm,
+    boundary_hbm,
+    send_hbm,
+    readout_hbm,
+    observed_hbm,
+    value_hbm,
+    var_hbm,
+    pert_hbm,
+    out_hbm,
     w_ref,
-    conn_ref,
-    sel_ref,
+    weight_ref,
+    index_ref,
+    boundary_ref,
+    send_ref,
     readout_ref,
     observed_ref,
     value_ref,
     var_ref,
     pert_ref,
-    out_hbm,
+    weight_pad,
+    index_pad,
+    conn_ref,
+    sel_ref,
+    small_sem,
     cur,
     noise,
     rate,
@@ -52,7 +70,9 @@
     members, vox, width = cur.shape
     steps = noise.shape[0]
     groups = members // group
-    block = group * cap
+    pseudo = group * parts
+    part = width // parts
+    block = pseudo * cap
     me = lax.axis_index("dom")
     mi = lax.axis_index("member")
     sib = mi + 1 - 2 * lax.rem(mi, 2)
@@ -71,7 +91,29 @@
     def noise_copy(k):
         return pltpu.make_async_copy(noise_hbm.at[k], noise.at[k], noise_sem.at[k])
 
-    for g in range(groups):
+    small = [
+        pltpu.make_async_copy(a, b, small_sem.at[i])
+        for i, (a, b) in enumerate(
+            (
+                (weight_hbm, weight_ref),
+                (index_hbm, index_ref),
+                (boundary_hbm, boundary_ref),
+                (send_hbm, send_ref),
+                (w_hbm, w_ref),
+                (readout_hbm, readout_ref),
+                (observed_hbm, observed_ref),
+                (value_hbm, value_ref),
+                (var_hbm, var_ref),
+                (pert_hbm, pert_ref),
+            )
+        )
+    ]
+    for copy in small[:4]:
+        copy.start()
+    state_copy(0).start()
+    for copy in small[4:]:
+        copy.start()
+    for g in range(1, groups):
         state_copy(g).start()
     for k in range(steps):
         noise_copy(k).start()
@@ -105,16 +147,74 @@
 
     order = sorted(range(1, n), key=lambda d: abs(2 * d - n))
 
+    for copy in small:
+        copy.wait()
+
+    wide_vox = weight_pad.shape[1]
+    halo_rows = n * block
+    index_pad[...] = jnp.full_like(index_pad, -1)
+    weight_pad[...] = jnp.zeros_like(weight_pad)
+    index_pad[:, 0:vox] = index_ref[...]
+    weight_pad[:, 0:vox] = weight_ref[...]
+    index = index_pad[...]
+    weight = weight_pad[...]
+    beyond = index - vox
+    slots = jnp.where(beyond < 0, -1 - halo_rows, (beyond // cap) * block + beyond % cap)
+    halo_iota = lax.broadcasted_iota(jnp.int32, (halo_rows, wide_vox), 0)
+    own_iota = lax.broadcasted_iota(jnp.int32, (wide_vox, wide_vox), 0)
+    own_lane = lax.broadcasted_iota(jnp.int32, (wide_vox, wide_vox), 1)
+    own = jnp.where(own_iota == own_lane, 1.0, 0.0)
+    for k in range(index.shape[0]):
+        own = own + jnp.where(own_iota == index[k : k + 1], weight[k : k + 1], 0.0)
+    own = own.T[:vox, :vox].astype(BF16)
+    for m in range(pseudo):
+        matrix = jnp.zeros((halo_rows, wide_vox), F32)
+        for k in range(index.shape[0]):
+            target = slots[k : k + 1] + m * cap
+            matrix = matrix + jnp.where(halo_iota == target, weight[k : k + 1], 0.0)
+        conn_ref[m, :, 0:halo_rows] = matrix.T[:vox].astype(BF16)
+        conn_ref[m, :, halo_rows : halo_rows + vox] = own
+
+    mine = send_ref[me]
+    local = jnp.zeros((n, cap), jnp.int32)
+    for b in range(boundary_ref.shape[1]):
+        local = local + jnp.where(mine == b, boundary_ref[0:1, b : b + 1], 0)
+    spread = jnp.where(
+        lax.broadcasted_iota(jnp.int32, (cap, halo_rows), 1) % cap
+        == lax.broadcasted_iota(jnp.int32, (cap, halo_rows), 0),
+        1.0,
+        0.0,
+    )
+    spread = jnp.dot(
+        local.astype(F32), spread, precision=HIGHEST, preferred_element_type=F32
+    )
+    mine_row = lax.broadcasted_iota(jnp.int32, (n, halo_rows), 1) // block
+    spread = jnp.where(
+        mine_row == lax.broadcasted_iota(jnp.int32, (n, halo_rows), 0), spread, 0.0
+    )
+    source_row = jnp.sum(spread, axis=0, keepdims=True)
+    lane = lax.broadcasted_iota(jnp.int32, (wide_vox, halo_rows), 1)
+    lane_member = (lane % block) // cap
+    voxel = lax.broadcasted_iota(jnp.int32, (wide_vox, halo_rows), 0).astype(F32)
+    chosen = jnp.where(voxel == source_row, 1.0, 0.0)
+    for m in range(pseudo):
+        matrix = jnp.where(lane_member == m, chosen, 0.0)
+        sel_ref[:, m * vox : (m + 1) * vox] = matrix.T[:, :vox].astype(BF16)
+
     def make_rate(g):
         rows = pl.ds(g * group, group)
         rate[rows] = jnp.tanh(cur[rows]).astype(BF16)
 
+    def pieces(g):
+        for h in range(parts):
+            for m in range(group):
+                yield rate[g * group + m, :, h * part : (h + 1) * part]
+
     def send(g, slot):
-        rows = pl.ds(g * group, group)
         picked = jnp.dot(
-            sel_ref[...], rate[rows].reshape(group * vox, width), preferred_element_type=F32
-        )
-        sendbuf[g, slot] = picked.astype(BF16).reshape(n, block, width)
+            sel_ref[...], jnp.concatenate(list(pieces(g)), axis=0), preferred_element_type=F32
+        )
+        sendbuf[g, slot] = picked.astype(BF16).reshape(n, block, part)
         for d in order:
             halo_copy(g, slot, d).start()
         recvbuf[g, slot, me] = sendbuf[g, slot, me]
@@ -126,32 +226,26 @@
             halo_copy(g, slot, d).wait_send()
 
     def update(g, slot, k):
-        halo = recvbuf[g, slot].reshape(n * block, width)
-        for m in range(group):
-            i = g * group + m
-            table = jnp.concatenate([halo, rate[i]], axis=0)
-            inputs = jnp.dot(conn_ref[m], table, preferred_element_type=F32).astype(BF16)
-            mixed = jnp.dot(inputs, w_ref[...], preferred_element_type=F32)
-            cur[i] = 0.5 * (cur[i] + mixed) + noise[k, i].astype(F32)
-
-    for g in range(groups):
-        state_copy(g).wait()
-        make_rate(g)
-        if g == 0:
-            pl.semaphore_wait(barrier, n - 1 + nm - 1)
-        send(g, 0)
-
-    def step(k, carry):
-        slot = lax.rem(k, 2)
-        noise_copy(k).wait()
-        for g in range(groups):
-            receive(g, slot)
-            update(g, slot, k)
-            make_rate(g)
-            send(g, 1 - slot)
-        return carry
-
-    lax.fori_loop(0, steps - 1, step, 0)
+        halo = recvbuf[g, slot].reshape(halo_rows, part)
+        drives = [
+            jnp.dot(
+                conn_ref[i],
+                jnp.concatenate([halo, own_rows], axis=0),
+                preferred_element_type=F32,
+            ).astype(BF16)
+            for i, own_rows in enumerate(pieces(g))
+        ]
+        inputs = jnp.concatenate(
+            [
+                jnp.concatenate([drives[h * group + m] for h in range(parts)], axis=1)
+                for m in range(group)
+            ],
+            axis=0,
+        )
+        mixed = jnp.dot(inputs, w_ref[...], preferred_element_type=F32)
+        rows = pl.ds(g * group, group)
+        mixed = mixed.reshape(group, vox, width)
+        cur[rows] = 0.5 * (cur[rows] + mixed) + noise[k, rows].astype(F32)
 
     def ens_piece(dev, g, c):
         return ens.at[dev, g, :, pl.ds(c * chunk, chunk)]
@@ -199,12 +293,7 @@
     vox_iota = lax.broadcasted_iota(jnp.int32, (vox, lanes), 0).astype(F32) + 1.0
     pick = jnp.where(vox_iota == padded[2:3, :], 1.0, 0.0)
 
-    last = steps - 1
-    slot = last % 2
-    noise_copy(last).wait()
-    for g in range(groups):
-        receive(g, slot)
-        update(g, slot, last)
+    def finish(g):
         rows = pl.ds(g * group, group)
         ens[mi, g] = cur[rows].astype(BF16)
         for c in range(chunks):
@@ -215,6 +304,37 @@
         for m in range(group):
             seen = jnp.sum(cur[g * group + m] * readout_ref[...], axis=1, keepdims=True)
             images[mi, g * group + m, :] = jnp.sum(pick * seen, axis=0)
+
+    last = steps - 1
+    flight = 2 if groups % 2 == 0 else 1
+    for g in range(flight):
+        state_copy(g).wait()
+        make_rate(g)
+        if g == 0:
+            pl.semaphore_wait(barrier, n - 1 + nm - 1)
+        send(g, 0)
+    for k in range(steps):
+        noise_copy(k).wait()
+    for first in range(0, groups, flight):
+
+        def step(k, carry):
+            slot = lax.rem(k, 2)
+            for g in range(first, first + flight):
+                receive(g, slot)
+                update(g, slot, k)
+                make_rate(g)
+                send(g, 1 - slot)
+            return carry
+
+        lax.fori_loop(0, last, step, 0)
+        for g in range(first, first + flight):
+            receive(g, last % 2)
+            update(g, last % 2, last)
+            if g + flight < groups:
+                state_copy(g + flight).wait()
+                make_rate(g + flight)
+                send(g + flight, 0)
+            finish(g)
 
     def img_copy(d):
         return pltpu.make_async_remote_copy(
@@ -344,52 +464,49 @@
     steps = noise.shape[0]
     n = lax.axis_size("dom")
     nm = lax.axis_size("member")
-    me = lax.axis_index("dom")
     cap = send_pos.shape[2]
     obs = observed.shape[1]
-    group = max(1, min(members, 16 // cap))
+    parts = 2
+    group = max(1, 16 // (cap * parts))
     groups = members // group
-    block = group * cap
+    block = group * parts * cap
     chunk = 32
-
-    halo = conn_index - vox
-    slots = (halo // cap) * block + lax.rem(halo, cap)
-    column = jnp.arange(n * block + vox, dtype=jnp.int32)
-    member = jnp.arange(group, dtype=jnp.int32)
-    target = jnp.where(
-        (halo < 0)[:, None, :],
-        (conn_index + n * block)[:, None, :],
-        slots[:, None, :] + member[None, :, None] * cap,
-    )
-    conn = jnp.sum(
-        jnp.where(target[..., None] == column, conn_weight[:, None, :, None], 0.0), axis=0
-    )
-    own = (column[None, :] - n * block) == jnp.arange(vox, dtype=jnp.int32)[:, None]
-    conn = (conn + own[None].astype(F32)).astype(BF16)
-
-    mine = lax.dynamic_index_in_dim(send_pos, me, 0, keepdims=False)
-    which = jnp.arange(boundary.shape[1], dtype=jnp.int32)
-    local = jnp.sum(jnp.where(mine[..., None] == which, boundary[0], 0), axis=-1)
-    flat = jnp.arange(group * vox, dtype=jnp.int32)
-    sel = flat == local[:, None, :, None] + member[None, :, None, None] * vox
-    sel = sel.astype(BF16).reshape(n * block, group * vox)
-
-    vmem = pl.BlockSpec(memory_space=pltpu.VMEM)
-    anywhere = pl.BlockSpec(memory_space=pl.ANY)
+    wide_vox = -(-vox // 128) * 128
+    halo_rows = n * block
+
+    hbm = pl.BlockSpec(memory_space=pltpu.HBM)
+    small = (
+        w_local,
+        conn_weight,
+        conn_index,
+        boundary,
+        send_pos,
+        readout[None, :],
+        observed,
+        obs_value,
+        obs_var,
+        obs_pert,
+    )
     dma = pltpu.SemaphoreType.DMA
     chunks = vox // chunk
     lanes = -(-obs // 128) * 128
     return pl.pallas_call(
-        functools.partial(kernel, n, nm, group, cap, chunk),
+        functools.partial(kernel, n, nm, group, cap, chunk, parts),
         out_shape=jax.ShapeDtypeStruct(state.shape, F32),
-        in_specs=[anywhere, anywhere] + [vmem] * 8,
-        out_specs=anywhere,
-        scratch_shapes=[
+        in_specs=[hbm] * 12,
+        out_specs=pl.BlockSpec(memory_space=pl.ANY),
+        scratch_shapes=[pltpu.VMEM(x.shape, x.dtype) for x in small]
+        + [
+            pltpu.VMEM((conn_index.shape[0], wide_vox), F32),
+            pltpu.VMEM((conn_index.shape[0], wide_vox), jnp.int32),
+            pltpu.VMEM((group * parts, vox, halo_rows + vox), BF16),
+            pltpu.VMEM((halo_rows, group * parts * vox), BF16),
+            dma((len(small),)),
             pltpu.VMEM((members, vox, width), F32),
             pltpu.VMEM((steps, members, vox, width), BF16),
             pltpu.VMEM((members, vox, width), BF16),
-            pltpu.VMEM((groups, 2, n, block, width), BF16),
-            pltpu.VMEM((groups, 2, n, block, width), BF16),
+            pltpu.VMEM((groups, 2, n, block, width // parts), BF16),
+            pltpu.VMEM((groups, 2, n, block, width // parts), BF16),
             pltpu.VMEM((nm, groups, group, vox, width), BF16),
             pltpu.VMEM((nm, members, lanes), F32),
             pltpu.VMEM((8 + members, lanes), F32),
@@ -405,19 +522,12 @@
             dma((chunks,)),
         ],
         compiler_params=pltpu.CompilerParams(
-            collective_id=0, has_side_effects=True, vmem_limit_bytes=48 * 1024 * 1024
+            collective_id=0, has_side_effects=True, vmem_limit_bytes=62 * 1024 * 1024
         ),
     )(
         state,
         noise,
-        w_local,
-        conn,
-        sel,
-        readout[None, :],
-        observed,
-        obs_value,
-        obs_var,
-        obs_pert,
+        *small,
     )
 
 

time: 95.1 us -> 113 us (1.19)
  Pallas kernels: 82.1 us -> 108 us
  other arithmetic: 4.66 us -> 0 us
  local copies, waits for them, and re-layouts: 7.82 us -> 4.11 us
    pallas_call x1, Pallas kernels: 82.1 us -> 108 us  [per_device(): pl.pallas_call(functools.partial(kernel, n, nm, group, cap, chunk, parts)...]
    unnamed x17 -> x2, local copies, waits for them, and re-layouts: 7.63 us -> 4.11 us
    reduce_sum x2 -> x0, other arithmetic: 2.96 us -> none  [the longest x1 2.09 us: per_device(): jnp.sum(jnp.where(target[..., None] == column, conn_weight[:, None, :, No...]
where the time goes in v2:
time: 113 us; the launch traced here: 112 us
  Pallas kernels  108 us (96%)
  local copies, waits for them, and re-layouts  4.11 us (4%)
    pallas_call x1, Pallas kernels, per_device(): pl.pallas_call(functools.partial(kernel, n, nm, group, cap, chunk, parts)...  108 us
    unnamed x2, local copies, waits for them, and re-layouts  4.11 us

profile of v2, /device:TPU:0, one launch (start us, length us, event | category | flops | bytes accessed | tf_op | source)
XLA Modules:
  0.0 112.3 jit_solution(9268532813542290753)
XLA Ops:
  0.0 1.4 %copy.13.send_hbm = s32[8,8,4]{2,1,0:T(8,128)} copy(s32[8,8,4]{1,2,0:T(4,128)} %param.18) | data formatting | bytes 2048 | tf_op args[6]
  1.4 108.1 %shard_map.118 = f32[8,96,512]{2,1,0:T(8,128)} custom-call(f32[8,96,512]{2,1,0:T(8,128)} %state_hbm.1, bf16[8,8,96,512]{3,2,1,0:T(8,128)(2,1)} %noise_hbm.1, bf16[512,512]{1,0:T(8,128)(2,1)} %w_hbm.1, f32[16,96]{1,0:T(8,128)} %weight_hbm.1, s32[16,96]{1,0:T(8,128)} %index_hbm.1, s32[1,8]{1,0:T(1,128)} %boundary_hbm.1, s32[8,8,4]{2,1,0:T(8,128)} %copy.13.send_hbm, ...), custom_call_target="tpu_custom_call" | custom-call | tf_op jit(solution)/shard_map/pallas_call | solution.py:493
  109.6 2.7 %copy.15 = f32[8,96,512]{2,1,0:T(8,128)} copy(f32[8,96,512]{2,1,0:T(8,128)} %shard_map.118) | data formatting | bytes 3145728

commit v3 on v2

--- a/solution.py
+++ b/solution.py
@@ -306,7 +306,7 @@
             images[mi, g * group + m, :] = jnp.sum(pick * seen, axis=0)
 
     last = steps - 1
-    flight = 2 if groups % 2 == 0 else 1
+    flight = groups
     for g in range(flight):
         state_copy(g).wait()
         make_rate(g)

time: 113 us -> 84.1 us (0.74)
  Pallas kernels: 108 us -> 79.7 us
    pallas_call x1, Pallas kernels: 108 us -> 79.7 us  [per_device(): pl.pallas_call(functools.partial(kernel, n, nm, group, cap, chunk, parts)...]
where the time goes in v3:
time: 84.1 us; the launch traced here: 83.8 us
  Pallas kernels  79.7 us (95%)
  local copies, waits for them, and re-layouts  4.11 us (5%)
    pallas_call x1, Pallas kernels, per_device(): pl.pallas_call(functools.partial(kernel, n, nm, group, cap, chunk, parts)...  79.7 us
    unnamed x2, local copies, waits for them, and re-layouts  4.11 us

profile of v3, /device:TPU:0, one launch (start us, length us, event | category | flops | bytes accessed | tf_op | source)
XLA Modules:
  0.0 83.8 jit_solution(4224626418155054149)
XLA Ops:
  0.0 1.4 %copy.13.send_hbm = s32[8,8,4]{2,1,0:T(8,128)} copy(s32[8,8,4]{1,2,0:T(4,128)} %param.18) | data formatting | bytes 2048 | tf_op args[6]
  1.4 79.7 %shard_map.118 = f32[8,96,512]{2,1,0:T(8,128)} custom-call(f32[8,96,512]{2,1,0:T(8,128)} %state_hbm.1, bf16[8,8,96,512]{3,2,1,0:T(8,128)(2,1)} %noise_hbm.1, bf16[512,512]{1,0:T(8,128)(2,1)} %w_hbm.1, f32[16,96]{1,0:T(8,128)} %weight_hbm.1, s32[16,96]{1,0:T(8,128)} %index_hbm.1, s32[1,8]{1,0:T(1,128)} %boundary_hbm.1, s32[8,8,4]{2,1,0:T(8,128)} %copy.13.send_hbm, ...), custom_call_target="tpu_custom_call" | custom-call | tf_op jit(solution)/shard_map/pallas_call | solution.py:493
  81.1 2.7 %copy.15 = f32[8,96,512]{2,1,0:T(8,128)} copy(f32[8,96,512]{2,1,0:T(8,128)} %shard_map.118) | data formatting | bytes 3145728
